TPU v7x, 32 devices: a whole 2x2x4 slice. The times are simulated.
32 devices in a mesh: dp: 8 (over z, x), key: 4 (over y, core).
Axes of the slice: x: 2, y: 2, z: 4, core: 2. Of those that a mesh axis runs over, the one named last changes fastest.
Arguments:
- ray_tokens: bfloat16 [16384, 768], P('dp'), may hold values from -6 to 6
- latents: bfloat16 [8, 4096, 768], P('dp', 'key'), may hold values from -6 to 6
- group_ids: int32 [8, 4096], P('dp', 'key'), may hold values from 0 to 15
- ln1_gain: bfloat16 [768], replicated, may hold values from 0.25 to 1.75
- ln1_shift: bfloat16 [768], replicated, may hold values from -3 to 3
- w_query: bfloat16 [768, 768], replicated, may hold values from -0.21875 to 0.21875
- w_key: bfloat16 [768, 768], replicated, may hold values from -0.21875 to 0.21875
- w_value: bfloat16 [768, 768], replicated, may hold values from -0.21875 to 0.21875
- w_out: bfloat16 [768, 768], replicated, may hold values from -6 to 6
- ln2_gain: bfloat16 [768], replicated, may hold values from 0.25 to 1.75
- ln2_shift: bfloat16 [768], replicated, may hold values from -3 to 3
- w_up: bfloat16 [768, 1536], replicated, may hold values from -0.21875 to 0.21875
- b_up: bfloat16 [1536], replicated, may hold values from -3 to 3
- w_down: bfloat16 [1536, 768], replicated, may hold values from -0.15625 to 0.15625
- b_down: bfloat16 [768], replicated, may hold values from -3 to 3
- intrinsics: bfloat16 [16, 768], replicated, may hold values from -3 to 3
- out_grad: bfloat16 [16384, 768], P(('dp', 'key')), may hold values from -6 to 6
Outputs:
- mixed: bfloat16 [16384, 768], P(('dp', 'key'))
- rays_grad: float32 [16384, 768], P(('dp', 'key'))
- latents_grad: float32 [8, 4096, 768], P('dp', 'key')
- ln1_gain_grad: float32 [768], replicated
- ln1_shift_grad: float32 [768], replicated
- w_query_grad: float32 [768, 768], replicated
- w_key_grad: float32 [768, 768], replicated
- w_value_grad: float32 [768, 768], replicated
- w_out_grad: float32 [768, 768], replicated
- ln2_gain_grad: float32 [768], replicated
- ln2_shift_grad: float32 [768], replicated
- w_up_grad: float32 [768, 1536], replicated
- b_up_grad: float32 [1536], replicated
- w_down_grad: float32 [1536, 768], replicated
- b_down_grad: float32 [768], replicated
- intrinsics_grad: float32 [16, 768], replicated
All inputs are finite; a program needn't handle non-finite values.
Results may differ from a plain program's by a relative error of at most 0.023.
Values may be sent and summed in bfloat16 or wider, within the bound.
No kernel may reach another device: no remote copies, remote signals or barrier semaphores. Data moves between devices by JAX's collectives and lax.ppermute only.
A program may use at most 192 MiB of HBM per device.

v0:
```python
import jax
import jax.numpy as jnp
from jax import lax
from jax.sharding import PartitionSpec as P

H = 12
HD = 64


EPSILON = 1e-05
HIGHEST = lax.Precision.HIGHEST


def norm_forward(values, gain_vec, shift_vec):
    centre = values - jnp.mean(values, axis=-1, keepdims=True)
    scaled = lax.rsqrt(jnp.mean(centre * centre, axis=-1, keepdims=True) + EPSILON)
    unit_rows = centre * scaled
    return (unit_rows * gain_vec + shift_vec, unit_rows, scaled)


def norm_backward(grad_rows, unit_rows, scaled, gain_vec):
    grad_unit = grad_rows * gain_vec
    centred_grad = (
        grad_unit
        - jnp.mean(grad_unit, axis=-1, keepdims=True)
        - unit_rows * jnp.mean(grad_unit * unit_rows, axis=-1, keepdims=True)
    )
    return (
        scaled * centred_grad,
        jnp.sum(grad_rows * unit_rows, axis=0),
        jnp.sum(grad_rows, axis=0),
    )


def block_scores(queries, key_heads):
    return jnp.einsum(
        "qhd,khd->hqk", queries, key_heads, preferred_element_type=jnp.float32
    ) * HD ** (-0.5)


def query_blocks(queries):
    row_count = queries.shape[0]
    block_rows = min(512, row_count)
    return queries.reshape(row_count // block_rows, block_rows, H, HD)


def score_blocks(queries, key_heads):
    return lax.map(
        lambda portion: jnp.max(block_scores(portion, key_heads), axis=-1), query_blocks(queries)
    )


def mix_blocks(queries, maxima, key_heads, value_heads):

    def mix_one(pieces):
        scores = block_scores(pieces[0], key_heads)
        exponent = jnp.exp(scores - pieces[1][:, :, None])
        blended = jnp.einsum(
            "hqk,khd->qhd",
            exponent.astype(jnp.bfloat16),
            value_heads,
            preferred_element_type=jnp.float32,
        )
        return (blended, jnp.transpose(jnp.sum(exponent, axis=-1)))

    blended, totals = lax.map(mix_one, (query_blocks(queries), maxima))
    row_count = queries.shape[0]
    return (blended.reshape(row_count, H * HD), totals.reshape(row_count, H))


def row_layout(maxima):
    return jnp.transpose(maxima, (0, 2, 1)).reshape(maxima.shape[0] * maxima.shape[2], H)


def attend_backward(queries, key_heads, value_heads, grad_heads, maxima, totals, deltas):
    row_count = queries.shape[0]
    block_rows = min(512, row_count)
    block_count = row_count // block_rows
    log_norm = maxima + jnp.log(totals)

    def step(carry, pieces):
        key_sum, value_sum = carry
        portion, grad_portion, norm_portion, delta_portion = pieces
        scores = block_scores(portion, key_heads)
        softmax_rows = jnp.exp(scores - jnp.transpose(norm_portion)[:, :, None])
        grad_probs = jnp.einsum(
            "qhd,khd->hqk", grad_portion, value_heads, preferred_element_type=jnp.float32
        )
        grad_scores = (
            softmax_rows * (grad_probs - jnp.transpose(delta_portion)[:, :, None])
        ).astype(jnp.bfloat16)
        grad_query = jnp.einsum(
            "hqk,khd->qhd", grad_scores, key_heads, preferred_element_type=jnp.float32
        ) * HD ** (-0.5)
        key_sum = key_sum + jnp.einsum(
            "hqk,qhd->khd", grad_scores, portion, preferred_element_type=jnp.float32
        ) * HD ** (-0.5)
        value_sum = value_sum + jnp.einsum(
            "hqk,qhd->khd",
            softmax_rows.astype(jnp.bfloat16),
            grad_portion,
            preferred_element_type=jnp.float32,
        )
        return ((key_sum, value_sum), grad_query)

    empty_sums = jnp.zeros(key_heads.shape, jnp.float32)
    (key_sum, value_sum), grad_query = lax.scan(
        step,
        (empty_sums, empty_sums),
        (
            queries.reshape(block_count, block_rows, H, HD),
            grad_heads.reshape(block_count, block_rows, H, HD),
            log_norm.reshape(block_count, block_rows, H),
            deltas.reshape(block_count, block_rows, H),
        ),
    )
    return (
        key_sum.reshape(key_heads.shape[0], H * HD),
        value_sum.reshape(key_heads.shape[0], H * HD),
        grad_query.reshape(row_count, H * HD),
    )


def local(
    ray_tokens,
    latents,
    group_ids,
    ln1_gain,
    ln1_shift,
    w_query,
    w_key,
    w_value,
    w_out,
    ln2_gain,
    ln2_shift,
    w_up,
    b_up,
    w_down,
    b_down,
    intrinsics,
    out_grad,
):
    share_rows = out_grad.shape[0]
    width = ray_tokens.shape[1]
    first_row = lax.axis_index("key") * share_rows
    gain_one = ln1_gain.astype(jnp.float32)
    shift_one = ln1_shift.astype(jnp.float32)
    gain_two = ln2_gain.astype(jnp.float32)
    shift_two = ln2_shift.astype(jnp.float32)
    lookup = (
        group_ids[0][:, None] == jnp.arange(intrinsics.shape[0], dtype=jnp.int32)[None, :]
    ).astype(jnp.float32)
    carried = (
        latents[0].astype(jnp.float32)
        + jnp.dot(lookup.astype(jnp.bfloat16), intrinsics, preferred_element_type=jnp.float32)
    ).astype(jnp.bfloat16)
    key_rows = jnp.dot(carried, w_key, preferred_element_type=jnp.float32).astype(jnp.bfloat16)
    value_rows = jnp.dot(carried, w_value, preferred_element_type=jnp.float32).astype(jnp.bfloat16)
    own_rays = lax.dynamic_slice_in_dim(ray_tokens, first_row, share_rows, 0).astype(jnp.float32)
    normed, unit_one, scale_one = norm_forward(ray_tokens.astype(jnp.float32), gain_one, shift_one)
    normed_low = normed.astype(jnp.bfloat16)
    queries = (
        jnp.dot(normed_low, w_query, preferred_element_type=jnp.float32)
        .astype(jnp.bfloat16)
        .reshape(-1, H, HD)
    )
    key_heads = key_rows.reshape(-1, H, HD)
    value_heads = value_rows.reshape(-1, H, HD)
    maxima = score_blocks(queries, key_heads)
    maxima = lax.pmax(maxima.astype(jnp.bfloat16), "key").astype(maxima.dtype)
    blended, totals = mix_blocks(queries, maxima, key_heads, value_heads)
    blended, totals = (
        lax.psum_scatter(
            blended.astype(jnp.bfloat16), "key", scatter_dimension=0, tiled=True
        ).astype(jnp.float32),
        lax.psum_scatter(
            totals.astype(jnp.bfloat16), "key", scatter_dimension=0, tiled=True
        ).astype(jnp.float32),
    )
    row_maxima = row_layout(maxima)
    own_normed = lax.dynamic_slice_in_dim(normed_low, first_row, share_rows, 0)
    own_unit = lax.dynamic_slice_in_dim(unit_one, first_row, share_rows, 0)
    own_scale = lax.dynamic_slice_in_dim(scale_one, first_row, share_rows, 0)
    attended = (blended.reshape(share_rows, H, HD) / totals[:, :, None]).reshape(share_rows, width)
    attended_low = attended.astype(jnp.bfloat16)
    middle = own_rays + jnp.dot(attended_low, w_out, preferred_element_type=jnp.float32)
    normed_two, unit_two, scale_two = norm_forward(middle, gain_two, shift_two)
    normed_two_low = normed_two.astype(jnp.bfloat16)
    hidden = jnp.dot(normed_two_low, w_up, preferred_element_type=jnp.float32) + b_up.astype(
        jnp.float32
    )
    active, gelu_back = jax.vjp(jax.nn.gelu, hidden)
    active_low = active.astype(jnp.bfloat16)
    result = (
        middle
        + jnp.dot(active_low, w_down, preferred_element_type=jnp.float32)
        + b_down.astype(jnp.float32)
    )
    output = result.astype(jnp.bfloat16)
    grad_out = out_grad.astype(jnp.float32)
    grad_active = lax.optimization_barrier(
        jnp.dot(out_grad, w_down.T, preferred_element_type=jnp.float32).astype(jnp.bfloat16)
    ).astype(jnp.float32)
    grad_hidden = gelu_back(grad_active)[0].astype(jnp.bfloat16)
    grad_w_down = jnp.dot(active_low.T, out_grad, preferred_element_type=jnp.float32)
    grad_b_down = jnp.sum(grad_out, axis=0)
    grad_w_up = jnp.dot(normed_two_low.T, grad_hidden, preferred_element_type=jnp.float32)
    grad_b_up = jnp.sum(grad_hidden.astype(jnp.float32), axis=0)
    grad_normed_two = jnp.dot(grad_hidden, w_up.T, preferred_element_type=jnp.float32)
    grad_middle_norm, grad_gain_two, grad_shift_two = norm_backward(
        grad_normed_two, unit_two, scale_two, gain_two
    )
    grad_middle = grad_out + grad_middle_norm
    grad_branch = grad_middle.astype(jnp.bfloat16)
    grad_w_out = jnp.dot(attended_low.T, grad_branch, preferred_element_type=jnp.float32)
    grad_attended = jnp.dot(grad_branch, w_out.T, preferred_element_type=jnp.float32).astype(
        jnp.bfloat16
    )
    deltas = jnp.sum(
        (grad_attended.astype(jnp.float32) * attended).reshape(share_rows, H, HD), axis=-1
    )
    branch_grads = (
        grad_w_out,
        grad_gain_two,
        grad_shift_two,
        grad_w_up,
        grad_b_up,
        grad_w_down,
        grad_b_down,
    )
    whole_grads = lax.all_gather(grad_attended, "key", axis=0, tiled=True)
    whole_totals, whole_deltas = (
        lax.all_gather(totals, "key", axis=0, tiled=True),
        lax.all_gather(deltas, "key", axis=0, tiled=True),
    )
    grad_key_sum, grad_value_sum, grad_query_part = attend_backward(
        queries,
        key_heads,
        value_heads,
        whole_grads.reshape(-1, H, HD),
        row_maxima,
        whole_totals,
        whole_deltas,
    )
    grad_queries = lax.psum_scatter(
        grad_query_part.astype(jnp.bfloat16), "key", scatter_dimension=0, tiled=True
    )
    grad_keys = grad_key_sum.astype(jnp.bfloat16)
    grad_values = grad_value_sum.astype(jnp.bfloat16)
    grad_w_query = jnp.dot(own_normed.T, grad_queries, preferred_element_type=jnp.float32)
    grad_normed = jnp.dot(grad_queries, w_query.T, preferred_element_type=jnp.float32)
    grad_rays_norm, grad_gain_one, grad_shift_one = norm_backward(
        grad_normed, own_unit, own_scale, gain_one
    )
    rays_grad = grad_middle + grad_rays_norm
    grad_w_key = jnp.dot(carried.T, grad_keys, preferred_element_type=jnp.float32)
    grad_w_value = jnp.dot(carried.T, grad_values, preferred_element_type=jnp.float32)
    grad_carried = jnp.dot(grad_keys, w_key.T, preferred_element_type=jnp.float32) + jnp.dot(
        grad_values, w_value.T, preferred_element_type=jnp.float32
    )
    grad_table = jnp.dot(lookup.T, grad_carried, precision=HIGHEST)
    summed = lax.psum(
        (
            grad_gain_one,
            grad_shift_one,
            grad_w_query,
            grad_w_key,
            grad_w_value,
            grad_table,
            branch_grads[0],
            branch_grads[1],
            branch_grads[2],
            branch_grads[3],
            branch_grads[4],
            branch_grads[5],
            branch_grads[6],
        ),
        ("dp", "key"),
    )
    attention_grads = summed[:6]
    branch_grads = summed[6:]
    return (
        output,
        rays_grad,
        grad_carried[None],
        attention_grads[0],
        attention_grads[1],
        attention_grads[2],
        attention_grads[3],
        attention_grads[4],
        branch_grads[0],
        branch_grads[1],
        branch_grads[2],
        branch_grads[3],
        branch_grads[4],
        branch_grads[5],
        branch_grads[6],
        attention_grads[5],
    )


def solution(mesh):
    placed = (
        P("dp", None),
        P("dp", "key", None),
        P("dp", "key"),
        P(),
        P(),
        P(),
        P(),
        P(),
        P(),
        P(),
        P(),
        P(),
        P(),
        P(),
        P(),
        P(),
        P(("dp", "key"), None),
    )
    return jax.shard_map(
        local,
        mesh=mesh,
        in_specs=placed,
        out_specs=(
            P(("dp", "key"), None),
            P(("dp", "key"), None),
            P("dp", "key", None),
            P(),
            P(),
            P(),
            P(),
            P(),
            P(),
            P(),
            P(),
            P(),
            P(),
            P(),
            P(),
            P(),
        ),
        check_vma=False,
    )
```

profile of v0, /device:TPU:0, one launch (start us, length us, event | category | flops | bytes accessed | tf_op | source)
XLA Modules:
  0.0 1061.3 jit_solution(13458874079183391105)
XLA Ops:
  39.4 20.9 %while.37 = (s32[]{:T(128)}, bf16[4,12,512]{2,1,0:T(8,128)(2,1)S(1)}, bf16[4,512,12,64]{1,3,2,0:T(8,128)(2,1)}, bf16[1024,12,64]{0,2,1:T(8,128)(2,1)}, s32[]{:T(128)}) while((s32[]{:T(128)}, bf16[4,12,512]{2,1,0:T(8,128)(2,1)S(1)}, bf16[4,512,12,64]{1,3,2,0:T(8,128)(2,1)}, bf16[1024,12,64]{0,2,1:T(8,128)(2,1)}, s32[]{:T(128)}) %tuple.104), condition=%wide.region_4.5_spmd, body=%wide.region_2.4_spmd.sunk | while | flops 817883136 | bytes 2404429 | solution.py:48
  60.4 13.7 %pmax.7 = bf16[4,12,512]{2,1,0:T(8,128)(2,1)S(1)} all-reduce(bf16[4,12,512]{2,1,0:T(8,128)(2,1)S(1)} %get-tuple-element.130), channel_id=1, replica_groups=mesh['dp'=8,'key'=4] {'key'}, use_global_device_ids=true, to_apply=%region_5.6 | all-reduce | flops 24576 | bytes 98304 | tf_op jit(solution)/shard_map/pmax | solution.py:170
  80.4 101.0 %while.38 = (s32[]{:T(128)}, bf16[4,512,12,64]{1,3,2,0:T(8,128)(2,1)}, bf16[4,512,12]{1,2,0:T(8,128)(2,1)S(1)}, bf16[4,512,12,64]{1,3,2,0:T(8,128)(2,1)}, bf16[1...) while((s32[]{:T(128)}, ...), condition=%wide.region_8.9_spmd, body=%wide.region_6.8_spmd.sunk | while | flops 1648355328 | bytes 87445704 | solution.py:66
  80.4 13.0 %fusion.126 = (bf16[12,512]{1,0:T(8,128)(2,1)S(1)}, f32[12,512,1024]{2,1,0:T(8,128)}) fusion(f32[12,512]{1,0:T(8,128)S(1)} %dynamic-slice_bitcast_fusion.2, bf16[1024,12,64]{0,2,1:T(8,128)(2,1)} %get-tuple-element.467, bf16[4,512,12,64]{1,3,2,0:T(8,128)(2,1)} %get-tuple-element.466, s32[]{:T(128)S(6)} %copy.85), kind=kOutput, calls=%fused_computation.6.clone.1 | convolution fusion | flops 824174592 | bytes 27561988 | tf_op jit(solution)/shard_map/while/body/eval_jaxpr/qhd,khd->hqk/dot_general | solution.py:36
  105.7 13.0 %fusion.126 = (bf16[12,512]{1,0:T(8,128)(2,1)S(1)}, f32[12,512,1024]{2,1,0:T(8,128)}) fusion(f32[12,512]{1,0:T(8,128)S(1)} %dynamic-slice_bitcast_fusion.2, bf16[1024,12,64]{0,2,1:T(8,128)(2,1)} %get-tuple-element.467, bf16[4,512,12,64]{1,3,2,0:T(8,128)(2,1)} %get-tuple-element.466, s32[]{:T(128)S(6)} %copy.85), kind=kOutput, calls=%fused_computation.6.clone.1 | convolution fusion | flops 824174592 | bytes 27561988 | tf_op jit(solution)/shard_map/while/body/eval_jaxpr/qhd,khd->hqk/dot_general | solution.py:36
  130.9 13.0 %fusion.126 = (bf16[12,512]{1,0:T(8,128)(2,1)S(1)}, f32[12,512,1024]{2,1,0:T(8,128)}) fusion(f32[12,512]{1,0:T(8,128)S(1)} %dynamic-slice_bitcast_fusion.2, bf16[1024,12,64]{0,2,1:T(8,128)(2,1)} %get-tuple-element.467, bf16[4,512,12,64]{1,3,2,0:T(8,128)(2,1)} %get-tuple-element.466, s32[]{:T(128)S(6)} %copy.85), kind=kOutput, calls=%fused_computation.6.clone.1 | convolution fusion | flops 824174592 | bytes 27561988 | tf_op jit(solution)/shard_map/while/body/eval_jaxpr/qhd,khd->hqk/dot_general | solution.py:36
  156.2 13.0 %fusion.126 = (bf16[12,512]{1,0:T(8,128)(2,1)S(1)}, f32[12,512,1024]{2,1,0:T(8,128)}) fusion(f32[12,512]{1,0:T(8,128)S(1)} %dynamic-slice_bitcast_fusion.2, bf16[1024,12,64]{0,2,1:T(8,128)(2,1)} %get-tuple-element.467, bf16[4,512,12,64]{1,3,2,0:T(8,128)(2,1)} %get-tuple-element.466, s32[]{:T(128)S(6)} %copy.85), kind=kOutput, calls=%fused_computation.6.clone.1 | convolution fusion | flops 824174592 | bytes 27561988 | tf_op jit(solution)/shard_map/while/body/eval_jaxpr/qhd,khd->hqk/dot_general | solution.py:36
  207.1 36.2 %reduce-scatter.4.cloned.1.call-done = bf16[512,768]{1,0:T(8,128)(2,1)} async-done(((bf16[2048,768]{1,0:T(8,128)(2,1)}), bf16[512,768]{1,0:T(8,128)(2,1)}) %reduce-scatter.4.cloned.1.call-update) | async-done | bytes 786448 | tf_op jit(solution)/shard_map/reduce_scatter | solution.py:173
  273.2 15.2 %all-gather.2.cloned.1.call-done = bf16[2048,768]{1,0:T(8,128)(2,1)} async-done(((bf16[512,768]{1,0:T(8,128)(2,1)}), bf16[2048,768]{1,0:T(8,128)(2,1)}) %all-gather.2.cloned.1.call-update) | async-done | bytes 3145744 | tf_op jit(solution)/shard_map/all_gather | solution.py:231
  305.5 235.5 %while.39 = (s32[]{:T(128)}, f32[1024,12,64]{0,2,1:T(8,128)}, f32[1024,12,64]{0,2,1:T(8,128)}, bf16[4,512,12,64]{1,3,2,0:T(8,128)(2,1)}, bf16[4,512,12,64]{1,3,2...) while((s32[]{:T(128)}, f32[1024,12,64]{0,2,1:T(8,128)}, ...), condition=%wide.region_17.18_spmd.clone, body=%wide.region_16.17_spmd.clone.sunk | while | flops 4081188864 | bytes 135536800 | solution.py:107
  305.7 11.3 %fusion.137 = f32[12,512,1024]{2,1,0:T(8,128)} fusion(bf16[1024,12,64]{0,2,1:T(8,128)(2,1)S(1)} %get-tuple-element.500, bf16[4,512,12,64]{1,3,2,0:T(8,128)(2,1)} %get-tuple-element.499, s32[]{:T(128)S(6)} %copy.95), kind=kOutput, calls=%fused_computation.29.clone.1 | convolution fusion | flops 805306368 | bytes 27525124 | tf_op jit(solution)/shard_map/while/body/eval_jaxpr/qhd,khd->hqk/dot_general | solution.py:36
  317.1 15.1 %multiply_convert_fusion.5 = bf16[12,512,1024]{2,1,0:T(8,128)(2,1)} fusion(f32[12,512,1024]{2,1,0:T(8,128)} %fusion.137, f32[12,512]{1,0:T(8,128)S(1)} %bitcast.190, f32[12,512]{1,0:T(8,128)S(1)} %bitcast.182, bf16[1024,12,64]{0,2,1:T(8,128)(2,1)} %get-tuple-element.503, bf16[4,512,12,64]{1,3,2,0:T(8,128)(2,1)} %get-tuple-element.502, s32[]{:T(128)S(6)} %copy.95), kind=kOutput, calls=%fused_computation.17.clone.1 | convolution fusion | flops 836763648 | bytes 40157188 | tf_op jit(solution)/shard_map/while/body/eval_jaxpr/qhd,khd->hqk/dot_general | solution.py:86
  341.0 12.8 %bitcast_add_fusion.5 = f32[1024,12,64]{0,2,1:T(8,128)} fusion(f32[1024,12,64]{0,2,1:T(8,128)} %get-tuple-element.485, f32[12,512,1024]{2,1,0:T(8,128)} %fusion.137, f32[12,512]{1,0:T(8,128)S(1)} %bitcast.183, pred[]{:T(512)S(6)} %compare.3, bf16[4,512,12,64]{1,3,2,0:T(8,128)(2,1)} %get-tuple-element.502, s32[]{:T(128)S(6)} %copy.95), kind=kOutput, calls=%fused_computation.23.clone.1 | convolution fusion | flops 825753600 | bytes 32268292 | tf_op jit(solution)/shard_map/while/body/eval_jaxpr/hqk,qhd->khd/dot_general | solution.py:98
  363.1 11.3 %fusion.137 = f32[12,512,1024]{2,1,0:T(8,128)} fusion(bf16[1024,12,64]{0,2,1:T(8,128)(2,1)S(1)} %get-tuple-element.500, bf16[4,512,12,64]{1,3,2,0:T(8,128)(2,1)} %get-tuple-element.499, s32[]{:T(128)S(6)} %copy.95), kind=kOutput, calls=%fused_computation.29.clone.1 | convolution fusion | flops 805306368 | bytes 27525124 | tf_op jit(solution)/shard_map/while/body/eval_jaxpr/qhd,khd->hqk/dot_general | solution.py:36
  374.5 15.1 %multiply_convert_fusion.5 = bf16[12,512,1024]{2,1,0:T(8,128)(2,1)} fusion(f32[12,512,1024]{2,1,0:T(8,128)} %fusion.137, f32[12,512]{1,0:T(8,128)S(1)} %bitcast.190, f32[12,512]{1,0:T(8,128)S(1)} %bitcast.182, bf16[1024,12,64]{0,2,1:T(8,128)(2,1)} %get-tuple-element.503, bf16[4,512,12,64]{1,3,2,0:T(8,128)(2,1)} %get-tuple-element.502, s32[]{:T(128)S(6)} %copy.95), kind=kOutput, calls=%fused_computation.17.clone.1 | convolution fusion | flops 836763648 | bytes 40157188 | tf_op jit(solution)/shard_map/while/body/eval_jaxpr/qhd,khd->hqk/dot_general | solution.py:86
  399.3 13.7 %bitcast_add_fusion.5 = f32[1024,12,64]{0,2,1:T(8,128)} fusion(f32[1024,12,64]{0,2,1:T(8,128)} %get-tuple-element.485, f32[12,512,1024]{2,1,0:T(8,128)} %fusion.137, f32[12,512]{1,0:T(8,128)S(1)} %bitcast.183, pred[]{:T(512)S(6)} %compare.3, bf16[4,512,12,64]{1,3,2,0:T(8,128)(2,1)} %get-tuple-element.502, s32[]{:T(128)S(6)} %copy.95), kind=kOutput, calls=%fused_computation.23.clone.1 | convolution fusion | flops 825753600 | bytes 32268292 | tf_op jit(solution)/shard_map/while/body/eval_jaxpr/hqk,qhd->khd/dot_general | solution.py:98
  422.4 11.3 %fusion.137 = f32[12,512,1024]{2,1,0:T(8,128)} fusion(bf16[1024,12,64]{0,2,1:T(8,128)(2,1)S(1)} %get-tuple-element.500, bf16[4,512,12,64]{1,3,2,0:T(8,128)(2,1)} %get-tuple-element.499, s32[]{:T(128)S(6)} %copy.95), kind=kOutput, calls=%fused_computation.29.clone.1 | convolution fusion | flops 805306368 | bytes 27525124 | tf_op jit(solution)/shard_map/while/body/eval_jaxpr/qhd,khd->hqk/dot_general | solution.py:36
  433.8 15.1 %multiply_convert_fusion.5 = bf16[12,512,1024]{2,1,0:T(8,128)(2,1)} fusion(f32[12,512,1024]{2,1,0:T(8,128)} %fusion.137, f32[12,512]{1,0:T(8,128)S(1)} %bitcast.190, f32[12,512]{1,0:T(8,128)S(1)} %bitcast.182, bf16[1024,12,64]{0,2,1:T(8,128)(2,1)} %get-tuple-element.503, bf16[4,512,12,64]{1,3,2,0:T(8,128)(2,1)} %get-tuple-element.502, s32[]{:T(128)S(6)} %copy.95), kind=kOutput, calls=%fused_computation.17.clone.1 | convolution fusion | flops 836763648 | bytes 40157188 | tf_op jit(solution)/shard_map/while/body/eval_jaxpr/qhd,khd->hqk/dot_general | solution.py:86
  458.6 13.7 %bitcast_add_fusion.5 = f32[1024,12,64]{0,2,1:T(8,128)} fusion(f32[1024,12,64]{0,2,1:T(8,128)} %get-tuple-element.485, f32[12,512,1024]{2,1,0:T(8,128)} %fusion.137, f32[12,512]{1,0:T(8,128)S(1)} %bitcast.183, pred[]{:T(512)S(6)} %compare.3, bf16[4,512,12,64]{1,3,2,0:T(8,128)(2,1)} %get-tuple-element.502, s32[]{:T(128)S(6)} %copy.95), kind=kOutput, calls=%fused_computation.23.clone.1 | convolution fusion | flops 825753600 | bytes 32268292 | tf_op jit(solution)/shard_map/while/body/eval_jaxpr/hqk,qhd->khd/dot_general | solution.py:98
  481.6 11.3 %fusion.137 = f32[12,512,1024]{2,1,0:T(8,128)} fusion(bf16[1024,12,64]{0,2,1:T(8,128)(2,1)S(1)} %get-tuple-element.500, bf16[4,512,12,64]{1,3,2,0:T(8,128)(2,1)} %get-tuple-element.499, s32[]{:T(128)S(6)} %copy.95), kind=kOutput, calls=%fused_computation.29.clone.1 | convolution fusion | flops 805306368 | bytes 27525124 | tf_op jit(solution)/shard_map/while/body/eval_jaxpr/qhd,khd->hqk/dot_general | solution.py:36
  493.0 15.1 %multiply_convert_fusion.5 = bf16[12,512,1024]{2,1,0:T(8,128)(2,1)} fusion(f32[12,512,1024]{2,1,0:T(8,128)} %fusion.137, f32[12,512]{1,0:T(8,128)S(1)} %bitcast.190, f32[12,512]{1,0:T(8,128)S(1)} %bitcast.182, bf16[1024,12,64]{0,2,1:T(8,128)(2,1)} %get-tuple-element.503, bf16[4,512,12,64]{1,3,2,0:T(8,128)(2,1)} %get-tuple-element.502, s32[]{:T(128)S(6)} %copy.95), kind=kOutput, calls=%fused_computation.17.clone.1 | convolution fusion | flops 836763648 | bytes 40157188 | tf_op jit(solution)/shard_map/while/body/eval_jaxpr/qhd,khd->hqk/dot_general | solution.py:86
  517.8 13.7 %bitcast_add_fusion.5 = f32[1024,12,64]{0,2,1:T(8,128)} fusion(f32[1024,12,64]{0,2,1:T(8,128)} %get-tuple-element.485, f32[12,512,1024]{2,1,0:T(8,128)} %fusion.137, f32[12,512]{1,0:T(8,128)S(1)} %bitcast.183, pred[]{:T(512)S(6)} %compare.3, bf16[4,512,12,64]{1,3,2,0:T(8,128)(2,1)} %get-tuple-element.502, s32[]{:T(128)S(6)} %copy.95), kind=kOutput, calls=%fused_computation.23.clone.1 | convolution fusion | flops 825753600 | bytes 32268292 | tf_op jit(solution)/shard_map/while/body/eval_jaxpr/hqk,qhd->khd/dot_general | solution.py:98
  603.8 113.7 %all-reduce.5.cloned.1.call-done = (f32[768]{0:T(1024)}, f32[768]{0:T(1024)}, f32[768]{0:T(1024)}, f32[768]{0:T(1024)}, f32[1536]{0:T(1024)}, /*index=5*/f32[768]{0:T(1024)}, f32[16,768]{1,0:T(8,128)}) async-done(((f32[768]{0:T(1024)}, f32[768]{0:T(1024)}, f32[768]{0:T(1024)}, f32[768]{0:T(1024)}, f32[1536]{0:T(1024)}, /*index=5*/f32[768]{0:T(1024)}, f32[16,768]{1,0:T(8,128)}), (f32[768]{0:T(1024)}, ...) | async-done | bytes 70672 | tf_op jit(solution)/shard_map/psum | solution.py:262
  717.5 317.0 %all-reduce.7.cloned.1.call-done = (f32[768,768]{1,0:T(8,128)}, f32[768,768]{1,0:T(8,128)}, f32[768,768]{1,0:T(8,128)}, f32[768,768]{1,0:T(8,128)}, f32[768,1536]{1,0:T(8,128)}, /*index=5*/f32[1536,768]{1,0:T(8,128)}) async-done(((f32[768,768]{1,0:T(8,128)}, f32[768,768]{1,0:T(8,128)}, f32[768,768]{1,0:T(8,128)}, f32[768,768]{1,0:T(8,128)}, f32[768,1536]{1,0:T(8,128)}, /*index=5*/f32[1536,768]{1,0:T(8,128)}), ...) | async-done | bytes 18874384 | tf_op jit(solution)/shard_map/psum | solution.py:262
  (297 shorter events, 338.1 us)
Async XLA Ops:
  7.2 239.7 %copy-start = (bf16[768,1536]{1,0:T(8,128)(2,1)S(1)}, bf16[768,1536]{1,0:T(8,128)(2,1)}, u32[]{:S(2)}) copy-start(bf16[768,1536]{1,0:T(8,128)(2,1)} %param.34) | copy-start | bytes 7077892
  7.2 194.8 %reduce-scatter.6.cloned.1.call-start = ((), (), s32[]{:S(2)}) async-start(), calls=%async_computation.4 | async-start | bytes 81920 | tf_op jit(solution)/shard_map/reduce_scatter | solution.py:176
  80.4 13.1 %copy-start.4 = (bf16[1024,12,64]{0,2,1:T(8,128)(2,1)S(1)}, bf16[1024,12,64]{0,2,1:T(8,128)(2,1)}, u32[]{:S(2)}) copy-start(bf16[1024,12,64]{0,2,1:T(8,128)(2,1)} %get-tuple-element.469) | copy-start | bytes 4718596 | tf_op jit(solution)/shard_map/while
  80.4 13.1 %copy-start.6 = (bf16[4,512,12,64]{1,3,2,0:T(8,128)(2,1)S(1)}, bf16[4,512,12,64]{1,3,2,0:T(8,128)(2,1)}, u32[]{:S(2)}) copy-start(bf16[4,512,12,64]{1,3,2,0:T(8,128)(2,1)} %get-tuple-element.456) | copy-start | bytes 9437188 | tf_op jit(solution)/shard_map/while
  105.7 13.1 %copy-start.4 = (bf16[1024,12,64]{0,2,1:T(8,128)(2,1)S(1)}, bf16[1024,12,64]{0,2,1:T(8,128)(2,1)}, u32[]{:S(2)}) copy-start(bf16[1024,12,64]{0,2,1:T(8,128)(2,1)} %get-tuple-element.469) | copy-start | bytes 4718596 | tf_op jit(solution)/shard_map/while
  105.7 13.1 %copy-start.6 = (bf16[4,512,12,64]{1,3,2,0:T(8,128)(2,1)S(1)}, bf16[4,512,12,64]{1,3,2,0:T(8,128)(2,1)}, u32[]{:S(2)}) copy-start(bf16[4,512,12,64]{1,3,2,0:T(8,128)(2,1)} %get-tuple-element.456) | copy-start | bytes 9437188 | tf_op jit(solution)/shard_map/while
  130.9 13.1 %copy-start.4 = (bf16[1024,12,64]{0,2,1:T(8,128)(2,1)S(1)}, bf16[1024,12,64]{0,2,1:T(8,128)(2,1)}, u32[]{:S(2)}) copy-start(bf16[1024,12,64]{0,2,1:T(8,128)(2,1)} %get-tuple-element.469) | copy-start | bytes 4718596 | tf_op jit(solution)/shard_map/while
  130.9 13.1 %copy-start.6 = (bf16[4,512,12,64]{1,3,2,0:T(8,128)(2,1)S(1)}, bf16[4,512,12,64]{1,3,2,0:T(8,128)(2,1)}, u32[]{:S(2)}) copy-start(bf16[4,512,12,64]{1,3,2,0:T(8,128)(2,1)} %get-tuple-element.456) | copy-start | bytes 9437188 | tf_op jit(solution)/shard_map/while
  156.2 13.1 %copy-start.4 = (bf16[1024,12,64]{0,2,1:T(8,128)(2,1)S(1)}, bf16[1024,12,64]{0,2,1:T(8,128)(2,1)}, u32[]{:S(2)}) copy-start(bf16[1024,12,64]{0,2,1:T(8,128)(2,1)} %get-tuple-element.469) | copy-start | bytes 4718596 | tf_op jit(solution)/shard_map/while
  156.2 13.1 %copy-start.6 = (bf16[4,512,12,64]{1,3,2,0:T(8,128)(2,1)S(1)}, bf16[4,512,12,64]{1,3,2,0:T(8,128)(2,1)}, u32[]{:S(2)}) copy-start(bf16[4,512,12,64]{1,3,2,0:T(8,128)(2,1)} %get-tuple-element.456) | copy-start | bytes 9437188 | tf_op jit(solution)/shard_map/while
  182.2 61.1 %reduce-scatter.4.cloned.1.call-start = ((), (), s32[]{:S(2)}) async-start(), calls=%async_computation.3 | async-start | bytes 3932160 | tf_op jit(solution)/shard_map/reduce_scatter | solution.py:173
  193.9 94.5 %all-gather.2.cloned.1.call-start = ((), (), s32[]{:S(2)}) async-start(), calls=%async_computation.5 | async-start | bytes 3932160 | tf_op jit(solution)/shard_map/all_gather | solution.py:231
  199.3 47.5 %copy-start.41 = (f32[768]{0:T(1024)}, f32[768]{0:T(1024)S(1)}, u32[]{:S(2)}) copy-start(f32[768]{0:T(1024)S(1)} %convert_element_type.161) | copy-start | bytes 9220
  199.3 55.4 %copy-start.35 = (f32[768]{0:T(1024)}, f32[768]{0:T(1024)S(1)}, u32[]{:S(2)}) copy-start(f32[768]{0:T(1024)S(1)} %convert_element_type.160) | copy-start | bytes 9220
  246.5 8.2 copy-start.8
  246.5 8.2 copy-start.31
  246.9 7.9 copy-start.37
  259.0 327.2 %reduce-scatter.8.cloned.1.call-start = ((), (), s32[]{:S(2)}) async-start(), calls=%async_computation.6 | async-start | bytes 3932160 | tf_op jit(solution)/shard_map/reduce_scatter | solution.py:245
  548.2 169.3 %all-reduce.5.cloned.1.call-start = ((), (), s32[]{:S(2)}) async-start(), calls=%async_computation.7 | async-start | bytes 155648 | tf_op jit(solution)/shard_map/psum | solution.py:262
  572.3 13.9 %copy-start.29 = (f32[768]{0:T(1024)S(1)}, f32[768]{0:T(1024)}, u32[]{:S(2)}) copy-start(f32[768]{0:T(1024)} %copy-done.28) | copy-start | bytes 9220
  572.3 13.9 %copy-start.56 = (bf16[768,768]{1,0:T(8,128)(2,1)S(1)}, bf16[768,768]{1,0:T(8,128)(2,1)}, u32[]{:S(2)}) copy-start(bf16[768,768]{1,0:T(8,128)(2,1)} %param.28) | copy-start | bytes 3538948
  590.9 443.5 %all-reduce.7.cloned.1.call-start = ((), (), s32[]{:S(2)}) async-start(), calls=%async_computation.8 | async-start | bytes 37748736 | tf_op jit(solution)/shard_map/psum | solution.py:262
  1040.4 7.2 slice-start.2
  1041.8 5.8 slice-start.3
  (58 other events, 183.8 us)
Sparse Core Ops, SparseCore 0:
  182.3 19.7 reduce-scatter.5
  205.3 37.9 reduce-scatter.3
  259.1 29.2 all-gather.1
  548.2 37.9 reduce-scatter.7
  594.8 122.6 all-reduce.4
  724.9 309.5 all-reduce.6
where the time goes:
time: 1070 us; the launch traced here: 1060 us
  waiting for transfers between devices  496 us (46%)
  matrix products  415 us (39%)
  local copies, waits for them, and re-layouts  94.1 us (9%)
  blocking collectives  25.2 us (2%)
  between operations  15.3 us (1%)
  other arithmetic  14.3 us (1%)
    psum x2, waiting for transfers between devices, local(): lax.psum((grad_gain_one, grad_shift_one, grad_w_query, grad_w_key, grad_w...  431 us
    dot_general x12, matrix products, block_scores(): jnp.einsum('qhd,khd->hqk', queries, key_heads, preferred_element_type=jnp...  118 us
    dot_general x4, matrix products, step(): jnp.einsum('qhd,khd->hqk', grad_portion, value_heads, preferred_element_t...  60.5 us
    dot_general x4, matrix products, step(): jnp.einsum('hqk,qhd->khd', softmax_rows.astype(jnp.bfloat16), grad_portio...  53.7 us
    dot_general x4, matrix products, mix_one(): jnp.einsum('hqk,khd->qhd', exponent.astype(jnp.bfloat16), value_heads, pr...  42 us
    dot_general x4, matrix products, step(): jnp.einsum('hqk,qhd->khd', grad_scores, portion, preferred_element_type=j...  37.9 us
    dot_general x4, matrix products, step(): jnp.einsum('hqk,khd->qhd', grad_scores, key_heads, preferred_element_type...  37.5 us
    reduce_scatter x1, waiting for transfers between devices, local(): lax.psum_scatter(blended.astype(jnp.bfloat16), 'key', scatter_dimension=0...  36.2 us
  transfers between devices with their start and end apart: 6, of which 6 were waited for; matrix products, arithmetic and copies ran while one was open for 6% of the time, Pallas kernels for 0%

commit v1 on v0

v1 whole, which is shorter than its diff:
```python
import functools

import jax
import jax.numpy as jnp
from jax import lax
from jax.experimental import pallas as pl
from jax.experimental.pallas import tpu as pltpu
from jax.sharding import PartitionSpec as P

H = 12
HD = 64
PAIR = 2 * HD
EPSILON = 1e-05
HIGHEST = lax.Precision.HIGHEST
BF = jnp.bfloat16
F32 = jnp.float32
LOG2E = 1.4426950408889634
LN2 = 0.6931471805599453
VMEM = 60 * 1024 * 1024


def dot(a, b, dims=((1,), (0,))):
    return lax.dot_general(a, b, (dims, ((), ())), preferred_element_type=F32)


NT = ((1,), (1,))
TN = ((0,), (0,))


def params(**kw):
    return pltpu.CompilerParams(vmem_limit_bytes=VMEM, **kw)


def head_half(x, h, axis=1):
    i = lax.broadcasted_iota(jnp.int32, x.shape, axis)
    return jnp.where((i < HD) == (h == 0), x, jnp.zeros_like(x))


def norm_forward(values, gain_vec, shift_vec):
    centre = values - jnp.mean(values, axis=-1, keepdims=True)
    scaled = lax.rsqrt(jnp.mean(centre * centre, axis=-1, keepdims=True) + EPSILON)
    unit_rows = centre * scaled
    return (unit_rows * gain_vec + shift_vec, unit_rows, scaled)


def norm_backward(grad_rows, unit_rows, scaled, gain_vec):
    grad_unit = grad_rows * gain_vec
    centred_grad = (
        grad_unit
        - jnp.mean(grad_unit, axis=-1, keepdims=True)
        - unit_rows * jnp.mean(grad_unit * unit_rows, axis=-1, keepdims=True)
    )
    return (
        scaled * centred_grad,
        jnp.sum(grad_rows * unit_rows, axis=0),
        jnp.sum(grad_rows, axis=0),
    )


def query_kernel(order, rays, gain, shift, wq, normed, q):
    n, _, _ = norm_forward(rays[...].astype(F32), gain[...].astype(F32), shift[...].astype(F32))
    n = n.astype(BF)
    normed[...] = n
    q[...] = (dot(n, wq[...]) * (HD**-0.5 * LOG2E)).astype(BF)


def query_call(order, core, rays, gain, shift, wq, share):
    rows, width = rays.shape
    cols = width // 2
    blocks = rows // share
    pre = jnp.concatenate([order, core[None]])
    return pl.pallas_call(
        query_kernel,
        grid_spec=pltpu.PrefetchScalarGridSpec(
            num_scalar_prefetch=1,
            grid=(blocks,),
            in_specs=[
                pl.BlockSpec((share, width), lambda i, o: (o[i], 0)),
                pl.BlockSpec((1, width), lambda i, o: (0, 0)),
                pl.BlockSpec((1, width), lambda i, o: (0, 0)),
                pl.BlockSpec((width, cols), lambda i, o: (0, o[blocks])),
            ],
            out_specs=[
                pl.BlockSpec((share, width), lambda i, o: (i, 0)),
                pl.BlockSpec((share, cols), lambda i, o: (i, 0)),
            ],
        ),
        out_shape=[
            jax.ShapeDtypeStruct((rows, width), BF),
            jax.ShapeDtypeStruct((rows, cols), BF),
        ],
        compiler_params=params(),
        name="rays_query",
    )(pre, rays, gain.reshape(1, -1), shift.reshape(1, -1), wq)


def keyval_kernel(core, x, wk, wv, k, v, kt, vt):
    kk = dot(x[...], wk[...])
    vv = dot(x[...], wv[...])
    k[...] = kk.astype(BF)
    v[...] = vv.astype(BF)
    kt[...] = kk.T.astype(BF)
    vt[...] = vv.T.astype(BF)


def keyval_call(core, carried, wk, wv):
    rows, width = carried.shape
    cols = width // 2
    blk = 512
    return pl.pallas_call(
        keyval_kernel,
        grid_spec=pltpu.PrefetchScalarGridSpec(
            num_scalar_prefetch=1,
            grid=(rows // blk,),
            in_specs=[
                pl.BlockSpec((blk, width), lambda i, o: (i, 0)),
                pl.BlockSpec((width, cols), lambda i, o: (0, o[0])),
                pl.BlockSpec((width, cols), lambda i, o: (0, o[0])),
            ],
            out_specs=[
                pl.BlockSpec((blk, cols), lambda i, o: (i, 0)),
                pl.BlockSpec((blk, cols), lambda i, o: (i, 0)),
                pl.BlockSpec((cols, blk), lambda i, o: (0, i)),
                pl.BlockSpec((cols, blk), lambda i, o: (0, i)),
            ],
        ),
        out_shape=[
            jax.ShapeDtypeStruct((rows, cols), BF),
            jax.ShapeDtypeStruct((rows, cols), BF),
            jax.ShapeDtypeStruct((cols, rows), BF),
            jax.ShapeDtypeStruct((cols, rows), BF),
        ],
        compiler_params=params(),
        name="keys_values",
    )(core[None], carried, wk, wv)


def attend_kernel(qb, qn, k, vt, o, st, e, s0, s1, mx, *, tc):
    i = pl.program_id(0)
    tokens = k.shape[0]
    rb = qb.shape[0]
    sb = (s0, s1)

    def score_chunk(dst, q, h, c, m):
        r = slice(c * tc, (c + 1) * tc)
        s = dot(head_half(k[r, :], h), q[...], NT)
        dst[r, :] = s
        mc = jnp.max(s.reshape(tc // 8, 8, rb), axis=0)
        return mc if m is None else jnp.maximum(m, mc)

    @pl.when(i == 0)
    def _():
        m = None
        for c in range(tokens // tc):
            m = score_chunk(s0, qb, 0, c, m)
        mx[0:1, :] = jnp.max(m, axis=0, keepdims=True)

    mixed = []
    for h in (0, 1):
        m = mx[h : h + 1, :]
        mn = None
        ot = None
        l = None
        for c in range(tokens // tc):
            r = slice(c * tc, (c + 1) * tc)
            mn = score_chunk(sb[1 - h], qb if h == 0 else qn, 1 - h, c, mn)
            p = jnp.exp2(sb[h][r, :] - m)
            lc = jnp.sum(p.reshape(tc // 8, 8, rb), axis=0)
            l = lc if l is None else l + lc
            pb = p.astype(BF)
            e[h, r, :] = pb
            oc = dot(vt[h * HD : (h + 1) * HD, r], pb)
            ot = oc if ot is None else ot + oc
        mx[1 - h : 2 - h, :] = jnp.max(mn, axis=0, keepdims=True)
        l = jnp.sum(l, axis=0, keepdims=True)
        mixed.append(ot / l)
        st[h : h + 1, :] = m
        st[h + 2 : h + 3, :] = m + jnp.log2(l)
    o[...] = jnp.concatenate(mixed, 0).T.astype(BF)


def attend_call(q, k, vt, p, rb=256):
    rays = q.shape[0]
    tokens = k.shape[0]
    n = rays // rb
    return pl.pallas_call(
        functools.partial(attend_kernel, tc=min(1024, tokens)),
        grid=(n,),
        in_specs=[
            pl.BlockSpec((rb, PAIR), lambda i: (i, p)),
            pl.BlockSpec((rb, PAIR), lambda i: (jnp.minimum(i + 1, n - 1), p)),
            pl.BlockSpec((tokens, PAIR), lambda i: (0, p)),
            pl.BlockSpec((PAIR, tokens), lambda i: (p, 0)),
        ],
        out_specs=[
            pl.BlockSpec((rb, PAIR), lambda i: (i, 0)),
            pl.BlockSpec((8, rb), lambda i: (0, i)),
            pl.BlockSpec((2, tokens, rb), lambda i: (0, 0, i)),
        ],
        out_shape=[
            jax.ShapeDtypeStruct((rays, PAIR), BF),
            jax.ShapeDtypeStruct((8, rays), F32),
            jax.ShapeDtypeStruct((2, tokens, rays), BF),
        ],
        scratch_shapes=[
            pltpu.VMEM((tokens, rb), F32),
            pltpu.VMEM((tokens, rb), F32),
            pltpu.VMEM((8, rb), F32),
        ],
        compiler_params=params(),
        cost_estimate=pl.CostEstimate(
            flops=16 * rays * tokens * PAIR, bytes_accessed=4 * rays * tokens, transcendentals=0
        ),
        name=f"attend_{p}",
    )(q, q, k, vt)


def spread(rows2):
    rows = rows2.shape[1]
    return jnp.concatenate([jnp.broadcast_to(rows2[h : h + 1, :], (HD, rows)) for h in (0, 1)], 0)


def combine_kernel(*refs, parts):
    os, sts = refs[:parts], refs[parts : 2 * parts]
    att, low, lse = refs[2 * parts :]
    ls = [s[2:4, :] for s in sts]
    top = functools.reduce(jnp.maximum, ls)
    tot = top + jnp.log2(sum(jnp.exp2(x - top) for x in ls))
    acc = 0.0
    for o, x in zip(os, ls):
        acc = acc + o[...].astype(F32) * spread(jnp.exp2(x - tot)).T
    att[...] = acc
    low[...] = acc.astype(BF)
    lse[0:2, :] = tot


def combine_call(os, sts, rows):
    parts = len(os)
    blk = 512 if rows % 512 == 0 else rows
    return pl.pallas_call(
        functools.partial(combine_kernel, parts=parts),
        grid=(rows // blk,),
        in_specs=[pl.BlockSpec((blk, PAIR), lambda i: (i, 0))] * parts
        + [pl.BlockSpec((8, blk), lambda i: (0, i))] * parts,
        out_specs=[
            pl.BlockSpec((blk, PAIR), lambda i: (i, 0)),
            pl.BlockSpec((blk, PAIR), lambda i: (i, 0)),
            pl.BlockSpec((8, blk), lambda i: (0, i)),
        ],
        out_shape=[
            jax.ShapeDtypeStruct((rows, PAIR), F32),
            jax.ShapeDtypeStruct((rows, PAIR), BF),
            jax.ShapeDtypeStruct((8, rows), F32),
        ],
        compiler_params=params(),
        name="combine",
    )(*os, *sts)


def delta_kernel(do, a0, a1, a2, out):
    for p, a in enumerate((a0, a1, a2)):
        prod = (do[:, p * PAIR : (p + 1) * PAIR].astype(F32) * a[...]).T
        for h in (0, 1):
            out[2 * p + h : 2 * p + h + 1, :] = jnp.sum(
                prod[h * HD : (h + 1) * HD, :], axis=0, keepdims=True
            )


def delta_call(do, atts):
    rows = do.shape[0]
    return pl.pallas_call(
        delta_kernel,
        out_shape=jax.ShapeDtypeStruct((8, rows), F32),
        compiler_params=params(),
        name="deltas",
    )(do, *atts)


def backward_kernel(e, do, q, st, lse, dl, kt, v, *refs, p, first):
    if first:
        dq, dk, dv = refs
    else:
        dk0, dv0, dq, dk, dv = refs

    @pl.when(pl.program_id(0) == 0)
    def _():
        if first:
            dk[...] = jnp.zeros_like(dk)
            dv[...] = jnp.zeros_like(dv)
        else:
            dk[...] = dk0[...]
            dv[...] = dv0[...]

    sc = jnp.exp2(st[0:2, :] - lse[0:2, :])
    scw = spread(sc)
    sct = scw.T
    dos = (do[...].astype(F32) * sct).astype(BF)
    qs = (q[...].astype(F32) * (sct * LN2)).astype(BF)
    grads = []
    for h in (0, 1):
        dp = dot(head_half(v[...], h), do[...], NT)
        grads.append((e[h].astype(F32) * (dp - dl[2 * p + h : 2 * p + h + 1, :])).astype(BF))
    dqt = jnp.concatenate(
        [dot(kt[h * HD : (h + 1) * HD, :], grads[h]) for h in (0, 1)], 0
    )
    dq[...] = (dqt * (scw * HD**-0.5)).T.astype(BF)
    both = lambda a: jnp.concatenate([head_half(a, 0), head_half(a, 1)], 0)
    dv[...] += dot(jnp.concatenate([e[0], e[1]], 1), both(dos))
    dk[...] += dot(jnp.concatenate(grads, 1), both(qs))


def backward_call(e, do, q, st, lse, dl, kt, v, carry, p, first_row, rb=256):
    rows = do.shape[0]
    tokens = v.shape[0]
    rb = min(rb, rows)
    off = first_row // rb
    whole = pl.BlockSpec((tokens, PAIR), lambda i: (0, 0))
    return pl.pallas_call(
        functools.partial(backward_kernel, p=p, first=carry is None),
        grid=(rows // rb,),
        in_specs=[
            pl.BlockSpec((2, tokens, rb), lambda i: (0, 0, i + off)),
            pl.BlockSpec((rb, PAIR), lambda i: (i, p)),
            pl.BlockSpec((rb, PAIR), lambda i: (i + off, p)),
            pl.BlockSpec((8, rb), lambda i: (0, i + off)),
            pl.BlockSpec((8, rb), lambda i: (0, i)),
            pl.BlockSpec((8, rb), lambda i: (0, i)),
            pl.BlockSpec((PAIR, tokens), lambda i: (p, 0)),
            pl.BlockSpec((tokens, PAIR), lambda i: (0, p)),
        ]
        + ([] if carry is None else [whole, whole]),
        out_specs=[pl.BlockSpec((rb, PAIR), lambda i: (i, 0)), whole, whole],
        out_shape=[
            jax.ShapeDtypeStruct((rows, PAIR), BF),
            jax.ShapeDtypeStruct((tokens, PAIR), F32),
            jax.ShapeDtypeStruct((tokens, PAIR), F32),
        ],
        compiler_params=params(),
        cost_estimate=pl.CostEstimate(
            flops=32 * rows * tokens * PAIR, bytes_accessed=4 * rows * tokens, transcendentals=0
        ),
        name=f"backward_{p}_{'own' if carry is None else 'far'}",
    )(e, do, q, st, lse, dl, kt, v, *(() if carry is None else carry))


def local(
    ray_tokens,
    latents,
    group_ids,
    ln1_gain,
    ln1_shift,
    w_query,
    w_key,
    w_value,
    w_out,
    ln2_gain,
    ln2_shift,
    w_up,
    b_up,
    w_down,
    b_down,
    intrinsics,
    out_grad,
    *,
    keys,
):
    share = out_grad.shape[0]
    width = ray_tokens.shape[1]
    cols = width // 2
    pairs = cols // PAIR
    chips = keys // 2
    chip_rows = 2 * share
    place = lax.axis_index("key")
    core = place % 2
    chip = place // 2

    def core_swap(x):
        return lax.ppermute(x, "key", [(i, i ^ 1) for i in range(keys)])

    def chip_shift(x, s):
        return lax.ppermute(x, "key", [(i, (i + 2 * s) % keys) for i in range(keys)])

    def own_cols(w):
        return lax.dynamic_slice_in_dim(w, core * cols, cols, 1)

    def far_cols(w):
        return lax.dynamic_slice_in_dim(w, (1 - core) * cols, cols, 1)

    def own_rows(w):
        return lax.dynamic_slice_in_dim(w, core * cols, cols, 0)

    def far_rows(w):
        return lax.dynamic_slice_in_dim(w, (1 - core) * cols, cols, 0)

    gain_one = ln1_gain.astype(F32)
    shift_one = ln1_shift.astype(F32)
    gain_two = ln2_gain.astype(F32)
    shift_two = ln2_shift.astype(F32)
    lookup = group_ids[0][:, None] == jnp.arange(intrinsics.shape[0], dtype=jnp.int32)[None, :]
    carried = (
        latents[0].astype(F32)
        + jnp.dot(lookup.astype(BF), intrinsics, preferred_element_type=F32)
    ).astype(BF)
    tokens = carried.shape[0]
    chip_carried = jnp.concatenate([carried, core_swap(carried)], 0)
    steps = jnp.arange(keys, dtype=jnp.int32)
    order = ((chip + steps // 2) % chips) * 2 + (core + steps % 2) % 2
    normed, queries = query_call(order, core, ray_tokens, ln1_gain, ln1_shift, w_query, share)
    key_rows, value_rows, key_cols, value_cols = keyval_call(core, chip_carried, w_key, w_value)

    stats, exps, atts, lows, lses = [], [], [], [], []
    for p in range(pairs):
        o, st, e = attend_call(queries, key_rows, value_cols, p)
        stats.append(st)
        exps.append(e)
        os, sts = [o], [st]
        for s in range(1, chips):
            os.append(chip_shift(o[s * chip_rows : (s + 1) * chip_rows], s))
            sts.append(chip_shift(st[:, s * chip_rows : (s + 1) * chip_rows], s))
        att, low, lse = combine_call(os, sts, chip_rows)
        atts.append(att)
        lows.append(low)
        lses.append(lse)
    low_chip = jnp.concatenate(lows, 1)
    low_own = low_chip[:share]
    low_far = core_swap(low_chip[share:])
    attended_low = jnp.concatenate(
        [jnp.where(core == 0, low_own, low_far), jnp.where(core == 0, low_far, low_own)], 1
    )
    own_rays = lax.dynamic_slice_in_dim(ray_tokens, place * share, share, 0).astype(F32)
    middle = own_rays + dot(attended_low, w_out)
    normed_two, unit_two, scale_two = norm_forward(middle, gain_two, shift_two)
    normed_two_low = normed_two.astype(BF)
    hidden = dot(normed_two_low, w_up) + b_up.astype(F32)
    active, gelu_back = jax.vjp(jax.nn.gelu, hidden)
    active_low = active.astype(BF)
    output = (middle + dot(active_low, w_down) + b_down.astype(F32)).astype(BF)
    grad_out = out_grad.astype(F32)
    grad_active = lax.optimization_barrier(dot(out_grad, w_down, NT).astype(BF)).astype(F32)
    grad_hidden = gelu_back(grad_active)[0].astype(BF)
    grad_normed_two = dot(grad_hidden, w_up, NT)
    grad_middle_norm, grad_gain_two, grad_shift_two = norm_backward(
        grad_normed_two, unit_two, scale_two, gain_two
    )
    grad_middle = grad_out + grad_middle_norm
    grad_branch = grad_middle.astype(BF)
    do_far = core_swap(dot(grad_branch, far_rows(w_out), NT).astype(BF))
    do_own = dot(grad_branch, own_rows(w_out), NT).astype(BF)
    do_chip = jnp.concatenate([do_own, do_far], 0)
    deltas = delta_call(do_chip, atts)
    dos, dls, lss = [do_chip], [deltas], [lses]
    for t in range(1, chips):
        dos.append(chip_shift(do_chip, chips - t))
        dls.append(chip_shift(deltas, chips - t))
        lss.append([chip_shift(x, chips - t) for x in lses])
    grad_w_down = dot(active_low, out_grad, TN)
    grad_b_down = jnp.sum(grad_out, axis=0)
    grad_w_up = dot(normed_two_low, grad_hidden, TN)
    grad_b_up = jnp.sum(grad_hidden.astype(F32), axis=0)
    grad_w_out = dot(attended_low, grad_branch, TN)

    grad_q, grad_k, grad_v = [], [], []
    for p in range(pairs):
        carry = None
        parts = []
        for t in range(chips):
            dq, dk, dv = backward_call(
                exps[p],
                dos[t],
                queries,
                stats[p],
                lss[t][p],
                dls[t],
                key_cols,
                value_rows,
                carry,
                p,
                t * chip_rows,
            )
            carry = (dk, dv)
            parts.append(dq if t == 0 else chip_shift(dq, t))
        grad_q.append(sum(x.astype(F32) for x in parts).astype(BF))
        grad_k.append(carry[0].astype(BF))
        grad_v.append(carry[1].astype(BF))
    grad_queries = jnp.concatenate(grad_q, 1)
    grad_keys = jnp.concatenate(grad_k, 1)
    grad_values = jnp.concatenate(grad_v, 1)
    grad_w_query = dot(normed[:chip_rows], grad_queries, TN)
    grad_w_key = dot(chip_carried, grad_keys, TN)
    grad_w_value = dot(chip_carried, grad_values, TN)
    keys_far = core_swap(grad_keys[tokens:])
    values_far = core_swap(grad_values[tokens:])
    queries_far = core_swap(grad_queries[share:])
    grad_carried = (
        dot(grad_keys[:tokens], own_cols(w_key), NT)
        + dot(keys_far, far_cols(w_key), NT)
        + dot(grad_values[:tokens], own_cols(w_value), NT)
        + dot(values_far, far_cols(w_value), NT)
    )
    grad_normed = dot(grad_queries[:share], own_cols(w_query), NT) + dot(
        queries_far, far_cols(w_query), NT
    )
    _, unit_one, scale_one = norm_forward(own_rays, gain_one, shift_one)
    grad_rays_norm, grad_gain_one, grad_shift_one = norm_backward(
        grad_normed, unit_one, scale_one, gain_one
    )
    rays_grad = grad_middle + grad_rays_norm
    grad_table = jnp.dot(lookup.astype(F32).T, grad_carried, precision=HIGHEST)
    whole = jnp.zeros((width, width), F32)
    put = lambda g: lax.dynamic_update_slice_in_dim(whole, g, core * cols, 1)
    big = (put(grad_w_query), put(grad_w_key), put(grad_w_value), grad_w_out, grad_w_up, grad_w_down)
    small = (grad_gain_one, grad_shift_one, grad_gain_two, grad_shift_two, grad_b_up, grad_b_down, grad_table)
    big = [x.astype(F32) for x in lax.psum([x.astype(BF) for x in big], ("dp", "key"))]
    small = lax.psum(small, ("dp", "key"))
    return (
        output,
        rays_grad,
        grad_carried[None],
        small[0],
        small[1],
        big[0],
        big[1],
        big[2],
        big[3],
        small[2],
        small[3],
        big[4],
        small[4],
        big[5],
        small[5],
        small[6],
    )


def solution(mesh):
    rows = P(("dp", "key"), None)
    placed = (P("dp", None), P("dp", "key", None), P("dp", "key")) + (P(),) * 13 + (rows,)
    return jax.shard_map(
        functools.partial(local, keys=mesh.shape["key"]),
        mesh=mesh,
        in_specs=placed,
        out_specs=(rows, rows, P("dp", "key", None)) + (P(),) * 13,
        check_vma=False,
    )
```

time: 1070 us -> 590 us (0.55)
  matrix products: 415 us -> 51.9 us
  waiting for transfers between devices: 496 us -> 284 us
  Pallas kernels: 0 us -> 148 us
  local copies, waits for them, and re-layouts: 94.1 us -> 35.6 us
  blocking collectives: 25.2 us -> 0 us
  starting transfers between devices: 0.65 us -> 16.7 us
  other arithmetic: 14.3 us -> 28.6 us
    dot_general x52 -> x21, matrix products: 415 us -> 51.9 us  [the longest x19 46.6 us: dot(): return lax.dot_general(a, b, (dims, ((), ())), preferred_element_type=F32)]
    pallas_call x0 -> x15, Pallas kernels: none -> 148 us  [the longest x6 77.4 us: backward_call(): pl.pallas_call(functools.partial(backward_kernel, p=p, first=carry is Non...]
    psum x2, waiting for transfers between devices: 431 us -> 284 us  [the longest x1 167 us: local(): lax.psum([x.astype(BF) for x in big], ('dp', 'key'))]
    reduce_scatter x3 -> x0, waiting for transfers between devices: 49.9 us -> none  [the longest x1 36.2 us: local(): lax.psum_scatter(blended.astype(jnp.bfloat16), 'key', scatter_dimension=0...]
    convert_element_type x5 -> x0, local copies, waits for them, and re-layouts: 18 us -> none  [the longest x2 8.97 us: local(): blended.astype(jnp.bfloat16)]
    another operation x5 -> x0, local copies, waits for them, and re-layouts: 17.1 us -> none  [the longest x1 6.15 us: attend_backward(): grad_heads.reshape(block_count, block_rows, H, HD)]
    ppermute x0 -> x20, starting transfers between devices: none -> 16.4 us  [the longest x14 15.1 us: chip_shift(): lax.ppermute(x, 'key', [(i, (i + 2 * s) % keys) for i in range(keys)])]
    all_gather x1 -> x0, waiting for transfers between devices: 15.2 us -> none  [local(): whole_grads = lax.all_gather(grad_attended, 'key', axis=0, tiled=True)]
  transfers between devices with their start and end apart: 6 -> 22, of which waited for: 6 -> 2; matrix products, arithmetic and copies ran while one was open for 6% -> 14% of each run, Pallas kernels for 0% -> 18%
where the time goes in v1:
time: 590 us; the launch traced here: 581 us
  waiting for transfers between devices  284 us (48%)
  Pallas kernels  148 us (25%)
  matrix products  51.9 us (9%)
  local copies, waits for them, and re-layouts  35.6 us (6%)
  other arithmetic  28.6 us (5%)
  starting transfers between devices  16.7 us (3%)
  between operations  15.3 us (3%)
    psum x1, waiting for transfers between devices, local(): lax.psum([x.astype(BF) for x in big], ('dp', 'key'))  167 us
    psum x1, waiting for transfers between devices, local(): small = lax.psum(small, ('dp', 'key'))  117 us
    pallas_call x6, Pallas kernels, backward_call(): pl.pallas_call(functools.partial(backward_kernel, p=p, first=carry is Non...  77.4 us
    pallas_call x3, Pallas kernels, attend_call(): pl.pallas_call(functools.partial(attend_kernel, tc=min(1024, tokens)), gr...  46.9 us
    dot_general x19, matrix products, dot(): return lax.dot_general(a, b, (dims, ((), ())), preferred_element_type=F32)  46.6 us
    unnamed x125, local copies, waits for them, and re-layouts  27.1 us
    ppermute x14, starting transfers between devices, chip_shift(): lax.ppermute(x, 'key', [(i, (i + 2 * s) % keys) for i in range(keys)])  15.1 us
    convert_element_type x6, other arithmetic, local(): x.astype(F32)  13 us
  transfers between devices with their start and end apart: 22, of which 2 were waited for; matrix products, arithmetic and copies ran while one was open for 14% of the time, Pallas kernels for 18%

profile of v1, /device:TPU:0, one launch (start us, length us, event | category | flops | bytes accessed | tf_op | source)
XLA Modules:
  0.0 581.0 jit_solution(10951682746917558602)
XLA Ops:
  7.3 3.4 fusion.10
  12.9 6.9 %rays_query.1 = (bf16[2048,768]{1,0:T(8,128)(2,1)}, bf16[2048,384]{1,0:T(8,128)(2,1)}) custom-call(s32[5]{0:T(128)} %pad_add_fusion.order, bf16[2048,768]{1,0:T(8,128)(2,1)} %rays.1, bf16[1,768]{1,0:T(2,128)(2,1)} %reshape.86.gain, bf16[1,768]{1,0:T(2,128)(2,1)} %reshape.87.shift, bf16[768,768]{1,0:T(8,128)(2,1)} %wq.1), custom_call_target="tpu_custom_call" | custom-call | tf_op jit(solution)/shard_map/rays_query/pallas_call | solution.py:72
  19.8 3.7 pad_maximum_fusion.x
  23.6 7.4 %keys_values.1 = (bf16[2048,384]{1,0:T(8,128)(2,1)}, bf16[2048,384]{1,0:T(8,128)(2,1)}, bf16[384,2048]{1,0:T(8,128)(2,1)}, bf16[384,2048]{1,0:T(8,128)(2,1)}) custom-call(s32[1]{0:T(128)} %bitcast.core, bf16[2048,768]{1,0:T(8,128)(2,1)} %pad_maximum_fusion.x, bf16[768,768]{1,0:T(8,128)(2,1)} %wk.1, bf16[768,768]{1,0:T(8,128)(2,1)} %wv.1), custom_call_target="tpu_custom_call" | custom-call | tf_op jit(solution)/shard_map/keys_values/pallas_call | solution.py:110
  31.0 15.5 %attend_0.1 = (bf16[2048,128]{1,0:T(8,128)(2,1)}, f32[8,2048]{1,0:T(8,128)}, bf16[2,2048,2048]{2,1,0:T(8,128)(2,1)}) custom-call(bf16[2048,384]{1,0:T(8,128)(2,1)} %get-tuple-element.58.qb.qn.q, bf16[2048,384]{1,0:T(8,128)(2,1)} %get-tuple-element.58.qb.qn.q, bf16[2048,384]{1,0:T(8,128)(2,1)} %get-tuple-element.59.k, bf16[384,2048]{1,0:T(8,128)(2,1)} %get-tuple-element.60.vt), custom_call_target="tpu_custom_call" | custom-call | flops 8589934592 | bytes 16777216 | tf_op jit(solution)/shard_map/attend_0/pallas_call | solution.py:186
  46.5 15.8 %attend_1.1 = (bf16[2048,128]{1,0:T(8,128)(2,1)}, f32[8,2048]{1,0:T(8,128)}, bf16[2,2048,2048]{2,1,0:T(8,128)(2,1)}) custom-call(bf16[2048,384]{1,0:T(8,128)(2,1)} %get-tuple-element.58.qb.qn.q, bf16[2048,384]{1,0:T(8,128)(2,1)} %get-tuple-element.58.qb.qn.q, bf16[2048,384]{1,0:T(8,128)(2,1)} %get-tuple-element.59.k, bf16[384,2048]{1,0:T(8,128)(2,1)} %get-tuple-element.60.vt), custom_call_target="tpu_custom_call" | custom-call | flops 8589934592 | bytes 16777216 | tf_op jit(solution)/shard_map/attend_1/pallas_call | solution.py:186
  69.4 15.6 %attend_2.1 = (bf16[2048,128]{1,0:T(8,128)(2,1)}, f32[8,2048]{1,0:T(8,128)}, bf16[2,2048,2048]{2,1,0:T(8,128)(2,1)}) custom-call(bf16[2048,384]{1,0:T(8,128)(2,1)} %get-tuple-element.58.qb.qn.q, bf16[2048,384]{1,0:T(8,128)(2,1)} %get-tuple-element.58.qb.qn.q, bf16[2048,384]{1,0:T(8,128)(2,1)} %get-tuple-element.59.k, bf16[384,2048]{1,0:T(8,128)(2,1)} %get-tuple-element.60.vt), custom_call_target="tpu_custom_call" | custom-call | flops 8589934592 | bytes 16777216 | tf_op jit(solution)/shard_map/attend_2/pallas_call | solution.py:186
  103.6 4.5 convolution_convert_fusion.2
  119.3 4.2 convert_reduce_fusion
  130.1 3.2 convolution_convert_fusion
  133.3 3.3 convolution_convert_fusion.1
  141.4 12.5 %backward_2_own.1 = (bf16[1024,128]{1,0:T(8,128)(2,1)}, f32[2048,128]{1,0:T(8,128)}, f32[2048,128]{1,0:T(8,128)}) custom-call(bf16[2,2048,2048]{2,1,0:T(8,128)(2,1)} %get-tuple-element.87.e, bf16[1024,384]{1,0:T(8,128)(2,1)} %copy-done.8, bf16[2048,384]{1,0:T(8,128)(2,1)} %get-tuple-element.58.qb.qn.q, f32[8,2048]{1,0:T(8,128)} %get-tuple-element.68.refs_2_.st, ...), custom_call_target="tpu_custom_call" | custom-call | flops 8589934592 | bytes 8388608 | tf_op jit(solution)/shard_map/backward_2_own/pallas_call | solution.py:318
  153.9 12.5 %backward_1_own.1 = (bf16[1024,128]{1,0:T(8,128)(2,1)}, f32[2048,128]{1,0:T(8,128)}, f32[2048,128]{1,0:T(8,128)}) custom-call(bf16[2,2048,2048]{2,1,0:T(8,128)(2,1)} %get-tuple-element.81.e, bf16[1024,384]{1,0:T(8,128)(2,1)} %copy-done.8, bf16[2048,384]{1,0:T(8,128)(2,1)} %get-tuple-element.58.qb.qn.q, f32[8,2048]{1,0:T(8,128)} %get-tuple-element.65.refs_2_.st, ...), custom_call_target="tpu_custom_call" | custom-call | flops 8589934592 | bytes 8388608 | tf_op jit(solution)/shard_map/backward_1_own/pallas_call | solution.py:318
  166.5 12.5 %backward_0_own.1 = (bf16[1024,128]{1,0:T(8,128)(2,1)}, f32[2048,128]{1,0:T(8,128)}, f32[2048,128]{1,0:T(8,128)}) custom-call(bf16[2,2048,2048]{2,1,0:T(8,128)(2,1)} %get-tuple-element.70.e, bf16[1024,384]{1,0:T(8,128)(2,1)} %copy-done.8, bf16[2048,384]{1,0:T(8,128)(2,1)} %get-tuple-element.58.qb.qn.q, f32[8,2048]{1,0:T(8,128)} %get-tuple-element.62.refs_2_.st, ...), custom_call_target="tpu_custom_call" | custom-call | flops 8589934592 | bytes 8388608 | tf_op jit(solution)/shard_map/backward_0_own/pallas_call | solution.py:318
  179.9 13.1 %backward_2_far.1 = (bf16[1024,128]{1,0:T(8,128)(2,1)}, f32[2048,128]{1,0:T(8,128)}, f32[2048,128]{1,0:T(8,128)}) custom-call(bf16[2,2048,2048]{2,1,0:T(8,128)(2,1)} %get-tuple-element.87.e, bf16[1024,384]{1,0:T(8,128)(2,1)} %copy-done.54, bf16[2048,384]{1,0:T(8,128)(2,1)} %get-tuple-element.58.qb.qn.q, f32[8,2048]{1,0:T(8,128)} %get-tuple-element.68.refs_2_.st, ...), custom_call_target="tpu_custom_call" | custom-call | flops 8589934592 | bytes 8388608 | tf_op jit(solution)/shard_map/backward_2_far/pallas_call | solution.py:318
  193.9 13.4 %backward_1_far.1 = (bf16[1024,128]{1,0:T(8,128)(2,1)}, f32[2048,128]{1,0:T(8,128)}, f32[2048,128]{1,0:T(8,128)}) custom-call(bf16[2,2048,2048]{2,1,0:T(8,128)(2,1)} %get-tuple-element.81.e, bf16[1024,384]{1,0:T(8,128)(2,1)} %copy-done.54, bf16[2048,384]{1,0:T(8,128)(2,1)} %get-tuple-element.58.qb.qn.q, f32[8,2048]{1,0:T(8,128)} %get-tuple-element.65.refs_2_.st, ...), custom_call_target="tpu_custom_call" | custom-call | flops 8589934592 | bytes 8388608 | tf_op jit(solution)/shard_map/backward_1_far/pallas_call | solution.py:318
  208.6 13.3 %backward_0_far.1 = (bf16[1024,128]{1,0:T(8,128)(2,1)}, f32[2048,128]{1,0:T(8,128)}, f32[2048,128]{1,0:T(8,128)}) custom-call(bf16[2,2048,2048]{2,1,0:T(8,128)(2,1)} %get-tuple-element.70.e, bf16[1024,384]{1,0:T(8,128)(2,1)} %copy-done.54, bf16[2048,384]{1,0:T(8,128)(2,1)} %get-tuple-element.58.qb.qn.q, f32[8,2048]{1,0:T(8,128)} %get-tuple-element.62.refs_2_.st, ...), custom_call_target="tpu_custom_call" | custom-call | flops 8589934592 | bytes 8388608 | tf_op jit(solution)/shard_map/backward_0_far/pallas_call | solution.py:318
  226.3 3.9 convolution_dynamic-update-slice_fusion.1
  230.3 4.1 convolution_dynamic-update-slice_fusion
  240.9 6.0 %add_convert_fusion = bf16[512,768]{1,0:T(8,128)(2,1)} fusion(f32[512,768]{1,0:T(8,128)} %copy-done.3, bf16[1536,768]{1,0:T(8,128)(2,1)} %param.30, f32[768]{0:T(1024)S(1)} %convert_element_type.152, f32[512,1536]{1,0:T(8,128)} %copy-done.57), kind=kOutput, calls=%fused_computation.46 | convolution fusion | flops 1216217088 | bytes 7867392 | tf_op jit(solution)/shard_map/dot_general | solution.py:23
  254.8 3.8 fusion.20
  262.7 3.3 fusion.19
  266.1 167.1 %all-reduce.7.cloned.1.call-done = (bf16[768,768]{1,0:T(8,128)(2,1)}, bf16[768,768]{1,0:T(8,128)(2,1)}, bf16[768,768]{1,0:T(8,128)(2,1)}, bf16[768,768]{1,0:T(8,...) async-done(((bf16[768,768]{1,0:T(8,128)(2,1)}, bf16[768,768]{1,0:T(8,128)(2,1)}, bf16[768,768]{1,0:T(8,128)(2,1)}, bf16[768,768]{1,0:T(8,128)(2,1)}, ...) | async-done | bytes 9437200 | tf_op jit(solution)/shard_map/psum | solution.py:513
  447.4 117.3 %all-reduce.5.cloned.1.call-done = (f32[768]{0:T(1024)}, f32[768]{0:T(1024)}, f32[768]{0:T(1024)}, f32[768]{0:T(1024)}, f32[1536]{0:T(1024)}, /*index=5*/f32[768]{0:T(1024)}, f32[16,768]{1,0:T(8,128)}) async-done(((f32[768]{0:T(1024)}, f32[768]{0:T(1024)}, f32[768]{0:T(1024)}, f32[768]{0:T(1024)}, f32[1536]{0:T(1024)}, /*index=5*/f32[768]{0:T(1024)}, f32[16,768]{1,0:T(8,128)}), (f32[768]{0:T(1024)}, ...) | async-done | bytes 70672 | tf_op jit(solution)/shard_map/psum | solution.py:514
  (239 shorter events, 99.4 us)
Async XLA Ops:
  7.2 110.5 %copy-start = (bf16[768,1536]{1,0:T(8,128)(2,1)S(1)}, bf16[768,1536]{1,0:T(8,128)(2,1)}, u32[]{:S(2)}) copy-start(bf16[768,1536]{1,0:T(8,128)(2,1)} %param.28) | copy-start | bytes 7077892
  7.2 426.0 %all-reduce.7.cloned.1.call-start = ((), (), s32[]{:S(2)}) async-start(), calls=%async_computation.1 | async-start | bytes 18874368 | tf_op jit(solution)/shard_map/psum | solution.py:513
  10.6 9.2 %collective-permute-start = (bf16[1024,768]{1,0:T(8,128)(2,1)}, bf16[1024,768]{1,0:T(8,128)(2,1)}, u32[]{:S(2)}, u32[]{:S(2)}) collective-permute-start(bf16[1024,768]{1,0:T(8,128)(2,1)} %fusion.10), channel_id=1, source_target_pairs={{0,1},{1,0},{2,3},{3,2},{4,5},{5,4},{6,7},{7,6},{8,9},{9,8},{10,11... | collective-permute-start | bytes 4718600 | tf_op jit(solution)/shard_map/ppermute | solution.py:378
  63.0 26.5 %collective-permute-start.1 = (bf16[1024,128]{1,0:T(8,128)(2,1)}, bf16[1024,128]{1,0:T(8,128)(2,1)S(1)}, u32[]{:S(2)}, u32[]{:S(2)}) collective-permute-start(bf16[1024,128]{1,0:T(8,128)(2,1)} %slice.45), channel_id=1, source_target_pairs={{0,2},{1,3},{2,0},{3,1},{4,6},{5,7},{6,4},{7,5},{8,10},{9,11},{10,... | collective-permute-start | bytes 786440 | tf_op jit(solution)/shard_map/ppermute | solution.py:381
  65.5 23.9 %collective-permute-start.2 = (f32[8,1024]{1,0:T(8,128)S(1)}, f32[8,1024]{1,0:T(8,128)S(1)}, u32[]{:S(2)}, u32[]{:S(2)}) collective-permute-start(f32[8,1024]{1,0:T(8,128)S(1)} %slice.46), channel_id=1, source_target_pairs={{0,2},{1,3},{2,0},{3,1},{4,6},{5,7},{6,4},{7,5},{8,10},{9,11},{10,... | collective-permute-start | bytes 98312 | tf_op jit(solution)/shard_map/ppermute | solution.py:381
  66.5 26.4 %collective-permute-start.3 = (bf16[1024,128]{1,0:T(8,128)(2,1)S(1)}, bf16[1024,128]{1,0:T(8,128)(2,1)S(1)}, u32[]{:S(2)}, u32[]{:S(2)}) collective-permute-start(bf16[1024,128]{1,0:T(8,128)(2,1)S(1)} %slice.47), channel_id=1, source_target_pairs={{0,2},{1,3},{2,0},{3,1},{4,6},{5,7},{6,4},{7,5},{8,10},{9,11},{10,... | collective-permute-start | bytes 786440 | tf_op jit(solution)/shard_map/ppermute | solution.py:381
  69.3 23.6 %collective-permute-start.4 = (f32[8,1024]{1,0:T(8,128)S(1)}, f32[8,1024]{1,0:T(8,128)S(1)}, u32[]{:S(2)}, u32[]{:S(2)}) collective-permute-start(f32[8,1024]{1,0:T(8,128)S(1)} %slice.48), channel_id=1, source_target_pairs={{0,2},{1,3},{2,0},{3,1},{4,6},{5,7},{6,4},{7,5},{8,10},{9,11},{10,... | collective-permute-start | bytes 98312 | tf_op jit(solution)/shard_map/ppermute | solution.py:381
  86.7 11.8 %collective-permute-start.5 = (bf16[1024,128]{1,0:T(8,128)(2,1)}, bf16[1024,128]{1,0:T(8,128)(2,1)S(1)}, u32[]{:S(2)}, u32[]{:S(2)}) collective-permute-start(bf16[1024,128]{1,0:T(8,128)(2,1)} %slice.49), channel_id=1, source_target_pairs={{0,2},{1,3},{2,0},{3,1},{4,6},{5,7},{6,4},{7,5},{8,10},{9,11},{10,... | collective-permute-start | bytes 786440 | tf_op jit(solution)/shard_map/ppermute | solution.py:381
  89.3 9.1 %collective-permute-start.6 = (f32[8,1024]{1,0:T(8,128)S(1)}, f32[8,1024]{1,0:T(8,128)S(1)}, u32[]{:S(2)}, u32[]{:S(2)}) collective-permute-start(f32[8,1024]{1,0:T(8,128)S(1)} %slice.50), channel_id=1, source_target_pairs={{0,2},{1,3},{2,0},{3,1},{4,6},{5,7},{6,4},{7,5},{8,10},{9,11},{10,... | collective-permute-start | bytes 98312 | tf_op jit(solution)/shard_map/ppermute | solution.py:381
  103.5 10.7 %collective-permute-start.7 = (bf16[512,384]{1,0:T(8,128)(2,1)S(1)}, bf16[512,384]{1,0:T(8,128)(2,1)}, u32[]{:S(2)}, u32[]{:S(2)}) collective-permute-start(bf16[512,384]{1,0:T(8,128)(2,1)S(1)} %slice.61), channel_id=1, source_target_pairs={{0,1},{1,0},{2,3},{3,2},{4,5},{5,4},{6,7},{7,6},{8,9},{9,8},{10,11... | collective-permute-start | bytes 1179656 | tf_op jit(solution)/shard_map/ppermute | solution.py:378
  110.7 68.3 %collective-permute-start.15 = (f32[8,1024]{1,0:T(8,128)}, f32[8,1024]{1,0:T(8,128)}, u32[]{:S(2)}, u32[]{:S(2)}) collective-permute-start(f32[8,1024]{1,0:T(8,128)} %get-tuple-element.88.lse), channel_id=1, source_target_pairs={{0,2},{1,3},{2,0},{3,1},{4,6},{5,7},{6,4},{7,5},{8,10},{9,11},{10,... | collective-permute-start | bytes 98312 | tf_op jit(solution)/shard_map/ppermute | solution.py:381
  112.2 81.7 %collective-permute-start.13 = (f32[8,1024]{1,0:T(8,128)}, f32[8,1024]{1,0:T(8,128)}, u32[]{:S(2)}, u32[]{:S(2)}) collective-permute-start(f32[8,1024]{1,0:T(8,128)} %get-tuple-element.82.lse), channel_id=1, source_target_pairs={{0,2},{1,3},{2,0},{3,1},{4,6},{5,7},{6,4},{7,5},{8,10},{9,11},{10,... | collective-permute-start | bytes 98312 | tf_op jit(solution)/shard_map/ppermute | solution.py:381
  112.8 95.8 %collective-permute-start.10 = (f32[8,1024]{1,0:T(8,128)}, f32[8,1024]{1,0:T(8,128)}, u32[]{:S(2)}, u32[]{:S(2)}) collective-permute-start(f32[8,1024]{1,0:T(8,128)} %get-tuple-element.71.lse), channel_id=1, source_target_pairs={{0,2},{1,3},{2,0},{3,1},{4,6},{5,7},{6,4},{7,5},{8,10},{9,11},{10,... | collective-permute-start | bytes 98312 | tf_op jit(solution)/shard_map/ppermute | solution.py:381
  129.4 7.1 %collective-permute-start.8 = (bf16[512,384]{1,0:T(8,128)(2,1)S(1)}, bf16[512,384]{1,0:T(8,128)(2,1)S(1)}, u32[]{:S(2)}, u32[]{:S(2)}) collective-permute-start(bf16[512,384]{1,0:T(8,128)(2,1)S(1)} %convolution_convert_fusion.4), channel_id=1, source_target_pairs={{0,1},{1,0},{2,3},{3,2},{4,5},{5,4},{6,7},{7,6},{8,9},{9,8},{10,11... | collective-permute-start | bytes 1179656 | tf_op jit(solution)/shard_map/ppermute | solution.py:378
  136.6 42.3 %collective-permute-start.9 = (bf16[1024,384]{1,0:T(8,128)(2,1)S(1)}, bf16[1024,384]{1,0:T(8,128)(2,1)S(1)}, u32[]{:S(2)}, u32[]{:S(2)}) collective-permute-start(bf16[1024,384]{1,0:T(8,128)(2,1)S(1)} %pad_maximum_fusion.4.do), channel_id=1, source_target_pairs={{0,2},{1,3},{2,0},{3,1},{4,6},{5,7},{6,4},{7,5},{8,10},{9,11},{10,... | collective-permute-start | bytes 2359304 | tf_op jit(solution)/shard_map/ppermute | solution.py:381
  140.2 38.8 %collective-permute-start.11 = (f32[8,1024]{1,0:T(8,128)}, f32[8,1024]{1,0:T(8,128)S(1)}, u32[]{:S(2)}, u32[]{:S(2)}) collective-permute-start(f32[8,1024]{1,0:T(8,128)} %deltas.1.dl), channel_id=1, source_target_pairs={{0,2},{1,3},{2,0},{3,1},{4,6},{5,7},{6,4},{7,5},{8,10},{9,11},{10,... | collective-permute-start | bytes 98312 | tf_op jit(solution)/shard_map/ppermute | solution.py:381
  193.0 41.4 %collective-permute-start.16 = (bf16[1024,128]{1,0:T(8,128)(2,1)}, bf16[1024,128]{1,0:T(8,128)(2,1)S(1)}, u32[]{:S(2)}, u32[]{:S(2)}) collective-permute-start(bf16[1024,128]{1,0:T(8,128)(2,1)} %get-tuple-element.92), channel_id=1, source_target_pairs={{0,2},{1,3},{2,0},{3,1},{4,6},{5,7},{6,4},{7,5},{8,10},{9,11},{10,... | collective-permute-start | bytes 786440 | tf_op jit(solution)/shard_map/ppermute | solution.py:381
  207.3 27.3 %collective-permute-start.14 = (bf16[1024,128]{1,0:T(8,128)(2,1)}, bf16[1024,128]{1,0:T(8,128)(2,1)S(1)}, u32[]{:S(2)}, u32[]{:S(2)}) collective-permute-start(bf16[1024,128]{1,0:T(8,128)(2,1)} %get-tuple-element.86), channel_id=1, source_target_pairs={{0,2},{1,3},{2,0},{3,1},{4,6},{5,7},{6,4},{7,5},{8,10},{9,11},{10,... | collective-permute-start | bytes 786440 | tf_op jit(solution)/shard_map/ppermute | solution.py:381
  221.9 12.7 %collective-permute-start.12 = (bf16[1024,128]{1,0:T(8,128)(2,1)}, bf16[1024,128]{1,0:T(8,128)(2,1)S(1)}, u32[]{:S(2)}, u32[]{:S(2)}) collective-permute-start(bf16[1024,128]{1,0:T(8,128)(2,1)} %get-tuple-element.80), channel_id=1, source_target_pairs={{0,2},{1,3},{2,0},{3,1},{4,6},{5,7},{6,4},{7,5},{8,10},{9,11},{10,... | collective-permute-start | bytes 786440 | tf_op jit(solution)/shard_map/ppermute | solution.py:381
  239.0 325.6 %all-reduce.5.cloned.1.call-start = ((), (), s32[]{:S(2)}) async-start(), calls=%async_computation | async-start | bytes 155648 | tf_op jit(solution)/shard_map/psum | solution.py:514
  250.7 4.1 collective-permute-start.17
  253.1 5.6 collective-permute-start.18
  253.2 6.6 %collective-permute-start.19 = (bf16[1024,384]{1,0:T(8,128)(2,1)S(1)}, bf16[1024,384]{1,0:T(8,128)(2,1)S(1)}, u32[]{:S(2)}, u32[]{:S(2)}) collective-permute-start(bf16[1024,384]{1,0:T(8,128)(2,1)S(1)} %slice.67), channel_id=1, source_target_pairs={{0,1},{1,0},{2,3},{3,2},{4,5},{5,4},{6,7},{7,6},{8,9},{9,8},{10,11... | collective-permute-start | bytes 2359304 | tf_op jit(solution)/shard_map/ppermute | solution.py:378
  444.8 128.9 %copy-start.1 = (bf16[768,1536]{1,0:T(8,128)(2,1)S(1)}, bf16[768,1536]{1,0:T(8,128)(2,1)}, u32[]{:S(2)}) copy-start(bf16[768,1536]{1,0:T(8,128)(2,1)} %param.28) | copy-start | bytes 7077892
  (56 other events, 216.2 us)
Sparse Core Ops, SparseCore 0:
  239.2 193.9 all-reduce.6
  441.9 122.7 all-reduce.4
